TPU v7x, 32 devices: a whole 2x2x4 slice. The times are simulated.
32 devices in a mesh: seq: 8 (over z, x), tp: 4 (over y, core).
Axes of the slice: x: 2, y: 2, z: 4, core: 2. Of those that a mesh axis runs over, the one named last changes fastest.
Arguments:
- tokens: bfloat16 [4096, 2304], P(('seq', 'tp')), may hold values from -6 to 6
- cotangent: bfloat16 [4096, 2304], P(('seq', 'tp')), may hold values from -6 to 6
- query_weight: bfloat16 [2304, 2048], P('seq', 'tp'), may hold values from -128 to 127, as said below
- key_weight: bfloat16 [2304, 1024], P('seq', 'tp'), may hold values from -128 to 127, as said below
- value_weight: bfloat16 [2304, 1024], P('seq', 'tp'), may hold values from -128 to 127, as said below
- output_weight: bfloat16 [2048, 2304], P('tp', 'seq'), may hold values from -128 to 127, as said below
- gate_weight: bfloat16 [2304, 9216], P('seq', 'tp'), may hold values from -128 to 127, as said below
- up_weight: bfloat16 [2304, 9216], P('seq', 'tp'), may hold values from -128 to 127, as said below
- down_weight: bfloat16 [9216, 2304], P('tp', 'seq'), may hold values from -128 to 127, as said below
- query_scale: float32 [2048], replicated, may hold values from 0 to 1, as said below
- key_scale: float32 [1024], replicated, may hold values from 0 to 1, as said below
- value_scale: float32 [1024], replicated, may hold values from 0 to 1, as said below
- output_scale: float32 [2304], replicated, may hold values from 0 to 1, as said below
- gate_scale: float32 [9216], replicated, may hold values from 0 to 1, as said below
- up_scale: float32 [9216], replicated, may hold values from 0 to 1, as said below
- down_scale: float32 [2304], replicated, may hold values from 0 to 1, as said below
- pre_attention: float32 [2304], replicated, may hold values from 0.25 to 1.75
- post_attention: float32 [2304], replicated, may hold values from 0.25 to 1.75
- pre_feedforward: float32 [2304], replicated, may hold values from 0.25 to 1.75
- post_feedforward: float32 [2304], replicated, may hold values from 0.25 to 1.75
- positions: int32 [4096], P('seq'), may hold values from 0 to 3584, as said below
Outputs:
- block_out: float32 [4096, 2304], P(('seq', 'tp'))
- token_grad: float32 [4096, 2304], P(('seq', 'tp'))
- query_grad: float32 [2304, 2048], P('seq', 'tp')
- key_grad: float32 [2304, 1024], P('seq', 'tp')
- value_grad: float32 [2304, 1024], P('seq', 'tp')
- output_grad: float32 [2048, 2304], P('tp', 'seq')
- gate_grad: float32 [2304, 9216], P('seq', 'tp')
- up_grad: float32 [2304, 9216], P('seq', 'tp')
- down_grad: float32 [9216, 2304], P('tp', 'seq')
- query_scale_grad: float32 [2048], replicated
- key_scale_grad: float32 [1024], replicated
- value_scale_grad: float32 [1024], replicated
- output_scale_grad: float32 [2304], replicated
- gate_scale_grad: float32 [9216], replicated
- up_scale_grad: float32 [9216], replicated
- down_scale_grad: float32 [2304], replicated
- pre_attention_grad: float32 [2304], replicated
- post_attention_grad: float32 [2304], replicated
- pre_feedforward_grad: float32 [2304], replicated
- post_feedforward_grad: float32 [2304], replicated
Inputs may be any that keep to these rules, and one draw needn't show every extreme that they name: `positions`: 0 at each document's first token and one more at each next token of it; one document runs from the first block of 512 tokens to the last and has exactly 3585 tokens. `query_weight`: whole numbers. `key_weight`: whole numbers. `value_weight`: whole numbers. `output_weight`: whole numbers. `gate_weight`: whole numbers. `up_weight`: whole numbers. `down_weight`: whole numbers. `query_scale`: positive. `key_scale`: positive. `value_scale`: positive. `output_scale`: positive. `gate_scale`: positive. `up_scale`: positive. `down_scale`: positive.
All inputs are finite; a program needn't handle non-finite values.
Results may differ from a plain program's by a relative error of at most 0.017.
Values may be sent and summed in bfloat16 or wider, within the bound.
No kernel may reach another device: no remote copies, remote signals or barrier semaphores. Data moves between devices by JAX's collectives and lax.ppermute only.
A program may use at most 256 MiB of HBM per device.

v0:
```python
import math

import jax
import jax.numpy as jnp
from jax import lax
from jax.experimental import pallas as pl
from jax.experimental.pallas import tpu as pltpu
from jax.sharding import Mesh
from jax.sharding import PartitionSpec as P

HEAD_DIM = 256
WINDOW = 4096
CAP = 50
EPSILON = 1e-06

EVERY = ("line", "pair", "row", "core")
SWAP = [(0, 1), (1, 0)]


def swapped(block, axis):
    return lax.ppermute(block, axis, SWAP)


def hop(block, distance, first):
    count = lax.axis_size("line")
    route = [(i, i + distance) for i in range(first, count) if 0 <= i + distance < count]
    return lax.ppermute(block, "line", route)


def put_together(sources, moves, shape):
    count = len(moves())
    if any(size % 16 for _, _, size, _, _ in moves()):
        out = jnp.zeros(shape, sources[0].dtype)
        for source, start, size, row, column in moves():
            piece = lax.dynamic_slice_in_dim(sources[source], start, size, 0)
            out = lax.dynamic_update_slice(out, piece, (row, column))
        return out

    def rows_at(row, size):
        return pl.ds(row if isinstance(row, int) else pl.multiple_of(row, 16), size)

    def kernel(*refs):
        out, sems = refs[len(sources)], refs[len(sources) + 1]
        copies = []
        for i, (source, start, size, row, column) in enumerate(moves()):
            piece = refs[source].at[rows_at(start, size)]
            target = out.at[rows_at(row, size), pl.ds(column, sources[source].shape[1])]
            copies.append(pltpu.make_async_copy(piece, target, sems.at[i]))
        for copy in copies:
            copy.start()
        for copy in copies:
            copy.wait()

    size = 2 * math.prod(shape) * sources[0].dtype.itemsize
    return pl.pallas_call(
        kernel,
        out_shape=jax.ShapeDtypeStruct(shape, sources[0].dtype),
        in_specs=[pl.BlockSpec(memory_space=pl.ANY)] * len(sources),
        out_specs=pl.BlockSpec(memory_space=pltpu.VMEM),
        scratch_shapes=[pltpu.SemaphoreType.DMA((count,))],
        compiler_params=pltpu.CompilerParams(vmem_limit_bytes=size // 2 + 4 * 1024 * 1024),
        cost_estimate=pl.CostEstimate(flops=0, bytes_accessed=size, transcendentals=0),
    )(*sources)


def tie(*values):
    return lax.optimization_barrier(values)


class Stream:
    def __init__(self, **blocks):
        self.blocks = blocks

    def stop(self, work, finish=(), start=()):
        here = [self.blocks[name] for name in finish]
        sources = [[self.blocks[name] for name in names] for _, names, _ in start]
        work, here, sources = tie(work, here, sources)
        self.blocks.update(zip(finish, here))
        for (name, _, route), blocks in zip(start, sources):
            self.blocks[name] = route(*blocks)
        return work


def nested_slice(codes):
    values = codes.astype(jnp.float32)
    return (jnp.clip(jnp.floor((values + 8.0) / 16.0), -8.0, 7.0) * 16.0).astype(jnp.bfloat16)


def inverse_rms(values):
    return lax.rsqrt(jnp.mean(values * values, axis=-1, keepdims=True) + EPSILON)


def norm_back(source, inverse, gain, upstream):
    scaled = upstream * gain
    inner = jnp.mean(scaled * source, axis=-1, keepdims=True)
    back = inverse * scaled - source * (inverse * inverse * inverse) * inner
    return (back, jnp.sum(upstream * source * inverse, axis=0))


def phases(positions):
    freqs = 10000.0 ** (-2.0 * jnp.arange(HEAD_DIM // 2, dtype=jnp.float32) / HEAD_DIM)
    angle = positions.astype(jnp.float32)[:, None] * freqs[None, :]
    return (jnp.cos(angle), jnp.sin(angle))


def rotate(values, cosine, sine):
    half = values.shape[-1] // 2
    first = values[..., :half]
    second = values[..., half:]
    return jnp.concatenate([first * cosine - second * sine, second * cosine + first * sine], -1)


def spread(piece, total, offset):
    return lax.dynamic_update_slice_in_dim(jnp.zeros((total,), jnp.float32), piece, offset, 0)


def in_order(mine, other, place):
    return lax.dynamic_slice_in_dim(
        jnp.concatenate([other, mine, other], 0), (1 - place) * mine.shape[0], 2 * mine.shape[0], 0
    )


def half_of(block, place):
    size = block.shape[1] // 2
    return lax.dynamic_slice_in_dim(block, place * size, size, 1)


def unstopped(work):
    return work


def gather8(block, with_halves=None, direct=False):
    size, width = block.shape
    cut = size // 2
    if direct:
        corner = lax.ppermute(block, ("pair", "row"), [(i, 3 - i) for i in range(4)])
        parts = [block, swapped(block, "row"), swapped(block, "pair"), corner]
        four = put_together(
            parts, lambda: [(i, 0, size, i * size, 0) for i in range(4)], (4 * size, width)
        )
        return put_together(
            [four, swapped(four, "core")],
            lambda: [(i, 0, 4 * size, i * 4 * size, 0) for i in range(2)],
            (8 * size, width),
        )
    left, right = block[:cut], block[cut:]
    left_p, right_r = swapped(left, "pair"), swapped(right, "row")
    left_r, right_p = swapped(left, "row"), swapped(right, "pair")
    left_pr, right_pr = swapped(left_p, "row"), swapped(right_r, "pair")
    halves = [left, right, left_r, right_r, left_p, right_p, left_pr, right_pr]
    four = put_together(
        halves, lambda: [(i, 0, cut, i * cut, 0) for i in range(8)], (4 * size, width)
    )
    other = swapped(four, "core")
    if with_halves is not None:
        four, other = with_halves(four, other)
    return put_together(
        [four, other],
        lambda: [(i, 0, 4 * size, i * 4 * size, 0) for i in range(2)],
        (8 * size, width),
    )


def summed(keep, got):
    return keep + got.astype(jnp.float32)


def sent(piece, axis):
    return swapped(piece.astype(jnp.bfloat16), axis)


def scatter8(terms, stop=unstopped):
    mine, others = terms
    size, width = mine.shape[0] // 4, mine.shape[1]
    mine, got = tie(mine, sent(others, "core"))
    four = stop(summed(mine, got)).reshape(2, 2, size, width)
    left, right = four[..., : width // 2], four[..., width // 2 :]
    left = summed(left[0], sent(left[1], "pair"))
    right = summed(right[:, 0], sent(right[:, 1], "row"))
    left = summed(left[0], sent(left[1], "row"))
    right = summed(right[0], sent(right[1], "pair"))
    return jnp.concatenate([left, right], 1)


def scatter8_last(terms, stop):
    mine, others = terms
    size, width = mine.shape[0] // 4, mine.shape[1]
    four = summed(mine, sent(others, "core")).reshape(2, 2, size, width)
    two = stop(summed(four[0], sent(four[1], "pair")))
    return summed(two[0], sent(two[1], "row"))


def blocks(rows, places):
    size = rows.shape[0] // len(places)
    return jnp.concatenate(
        [lax.dynamic_slice_in_dim(rows, place * size, size, 0) for place in places], 0
    )


def to_tokens(rows, pair, row, core):
    places = [
        ((c ^ core) * 4 + (p ^ pair) * 2 + (r ^ row))
        for p in range(2)
        for r in range(2)
        for c in range(2)
    ]
    return blocks(rows, places)


def from_tokens(rows, pair, row, core):
    places = [
        ((p ^ pair) * 4 + (r ^ row) * 2 + (c ^ core))
        for c in range(2)
        for p in range(2)
        for r in range(2)
    ]
    return blocks(rows, places)


def exchanged(vector, axis):
    if isinstance(axis, str):
        return swapped(vector, axis)
    count = lax.axis_size("line")
    return lax.ppermute(vector, "line", [(i, i ^ axis) for i in range(count)])


def across(left, right):
    return lax.dot_general(left, right, (((1,), (1,)), ((), ())), preferred_element_type=jnp.float32)

def attend(queries, keys, values, low, bq=512, bk=1024):
    rows, span = queries.shape[0], keys.shape[0]
    offset = span - rows
    first = jnp.min(low.reshape(rows // bq, bq), axis=1) // bk

    def kernel(first_ref, q_ref, k_ref, v_ref, low_ref, o_ref, lse_ref, sums, totals):
        block = pl.program_id(0)
        high = offset + block * bq + lax.broadcasted_iota(jnp.int32, (bq, 1), 0)
        sums[...] = jnp.zeros_like(sums)
        totals[...] = jnp.zeros_like(totals)

        def chunk(c, carry):
            at = pl.multiple_of(c * bk, bk)
            raw = across(q_ref[...], k_ref[pl.ds(at, bk), :])
            place = at + lax.broadcasted_iota(jnp.int32, (bq, bk), 1)
            seen = (place >= low_ref[...]) & (place <= high)
            expo = jnp.where(seen, jnp.exp(CAP * jnp.tanh(raw * (1.0 / CAP))), 0.0)
            totals[...] += jnp.sum(expo, axis=-1, keepdims=True)
            sums[...] += jnp.dot(expo.astype(jnp.bfloat16), v_ref[pl.ds(at, bk), :], preferred_element_type=jnp.float32)
            return carry

        lax.fori_loop(first_ref[block], (offset + (block + 1) * bq - 1) // bk + 1, chunk, 0)
        o_ref[...] = sums[...] / totals[...]
        lse_ref[...] = jnp.log(totals[...])

    whole = lambda i, *_: (0, 0)
    mine = lambda i, *_: (i, 0)
    return pl.pallas_call(
        kernel,
        out_shape=(jax.ShapeDtypeStruct((rows, HEAD_DIM), jnp.float32), jax.ShapeDtypeStruct((rows, 1), jnp.float32)),
        grid_spec=pltpu.PrefetchScalarGridSpec(
            num_scalar_prefetch=1, grid=(rows // bq,),
            in_specs=[pl.BlockSpec((bq, HEAD_DIM), mine), pl.BlockSpec((span, HEAD_DIM), whole), pl.BlockSpec((span, HEAD_DIM), whole), pl.BlockSpec((bq, 1), mine)],
            out_specs=(pl.BlockSpec((bq, HEAD_DIM), mine), pl.BlockSpec((bq, 1), mine)),
            scratch_shapes=[pltpu.VMEM((bq, HEAD_DIM), jnp.float32), pltpu.VMEM((bq, 1), jnp.float32)]),
        compiler_params=pltpu.CompilerParams(vmem_limit_bytes=40 * 1024 * 1024),
        cost_estimate=pl.CostEstimate(flops=4 * rows * span * HEAD_DIM, bytes_accessed=4 * span * HEAD_DIM, transcendentals=2 * rows * span),
    )(first, queries, keys, values, low)

def attend_back(queries, keys, values, low, lse, delta, upstream, bq=1024, bk=512):
    rows, span = queries.shape[0], keys.shape[0]
    offset = span - rows
    first = jnp.min(low.reshape(rows // bq, bq), axis=1) // bk

    def kernel(first_ref, q_ref, up_ref, k_ref, kt_ref, v_ref, low_ref, lse_ref, delta_ref, dq_ref, dk_ref, dv_ref):
        block = pl.program_id(0)
        high = offset + block * bq + lax.broadcasted_iota(jnp.int32, (1, bq), 1)

        @pl.when(block == 0)
        def clear():
            dk_ref[...] = jnp.zeros_like(dk_ref)
            dv_ref[...] = jnp.zeros_like(dv_ref)

        dq_ref[...] = jnp.zeros_like(dq_ref)

        def chunk(c, carry):
            at = pl.multiple_of(c * bk, bk)
            here = pl.ds(at, bk)
            ratio = jnp.tanh(across(k_ref[here, :], q_ref[...]) * (1.0 / CAP))
            place = at + lax.broadcasted_iota(jnp.int32, (bk, bq), 0)
            seen = (place >= low_ref[...]) & (place <= high)
            probs = jnp.where(seen, jnp.exp(CAP * ratio - lse_ref[...]), 0.0)
            dv_ref[here, :] += jnp.dot(probs.astype(jnp.bfloat16), up_ref[...], preferred_element_type=jnp.float32)
            dprobs = across(v_ref[here, :], up_ref[...])
            draw = (probs * (dprobs - delta_ref[...]) * (1.0 - ratio * ratio)).astype(jnp.bfloat16)
            dk_ref[here, :] += jnp.dot(draw, q_ref[...], preferred_element_type=jnp.float32)
            dq_ref[...] += jnp.dot(kt_ref[:, here], draw, preferred_element_type=jnp.float32)
            return carry

        lax.fori_loop(first_ref[block], (offset + (block + 1) * bq - 1) // bk + 1, chunk, 0)

    whole = lambda i, *_: (0, 0)
    mine = lambda i, *_: (i, 0)
    across_lanes = lambda i, *_: (0, i)
    return pl.pallas_call(
        kernel,
        out_shape=(jax.ShapeDtypeStruct((HEAD_DIM, rows), jnp.float32), jax.ShapeDtypeStruct((span, HEAD_DIM), jnp.float32), jax.ShapeDtypeStruct((span, HEAD_DIM), jnp.float32)),
        grid_spec=pltpu.PrefetchScalarGridSpec(
            num_scalar_prefetch=1, grid=(rows // bq,),
            in_specs=[pl.BlockSpec((bq, HEAD_DIM), mine), pl.BlockSpec((bq, HEAD_DIM), mine), pl.BlockSpec((span, HEAD_DIM), whole), pl.BlockSpec((HEAD_DIM, span), whole), pl.BlockSpec((span, HEAD_DIM), whole),
                      pl.BlockSpec((1, bq), across_lanes), pl.BlockSpec((1, bq), across_lanes), pl.BlockSpec((1, bq), across_lanes)],
            out_specs=(pl.BlockSpec((HEAD_DIM, bq), across_lanes), pl.BlockSpec((span, HEAD_DIM), whole), pl.BlockSpec((span, HEAD_DIM), whole))),
        compiler_params=pltpu.CompilerParams(vmem_limit_bytes=48 * 1024 * 1024),
        cost_estimate=pl.CostEstimate(flops=10 * rows * span * HEAD_DIM, bytes_accessed=12 * span * HEAD_DIM, transcendentals=2 * rows * span),
    )(first, queries, upstream, keys, keys.T, values, low.T, lse.T, delta.T)


def body(
    tokens,
    cotangent,
    query_weight,
    key_weight,
    value_weight,
    output_weight,
    gate_weight,
    up_weight,
    down_weight,
    query_scale,
    key_scale,
    value_scale,
    output_scale,
    gate_scale,
    up_scale,
    down_scale,
    pre_attention,
    post_attention,
    pre_feedforward,
    post_feedforward,
    positions,
):
    lines = lax.axis_size("line")
    line, pair = lax.axis_index("line"), lax.axis_index("pair")
    row, core = lax.axis_index("row"), lax.axis_index("core")
    tp_index = row * 2 + core
    scale = 1.0 / math.sqrt(HEAD_DIM)
    even = pair == 0
    qcols = query_weight.shape[1] // 2
    kcols = key_weight.shape[1]
    ocols = output_weight.shape[0] // 2
    fcols = gate_weight.shape[1] // 2
    rows = 8 * tokens.shape[0]

    wq, wk, wv, wo, wg, wu, wd = (
        nested_slice(query_weight),
        nested_slice(key_weight),
        nested_slice(value_weight),
        nested_slice(output_weight.T),
        nested_slice(gate_weight),
        nested_slice(up_weight),
        nested_slice(down_weight.T),
    )

    def paired(keep, give):
        return in_order(keep, swapped(give, "pair"), pair)

    def over_line(block):
        return lax.all_gather(block, "line", axis=0, tiled=True)

    def shared_out(shard):
        return paired(half_of(shard, pair), half_of(shard, 1 - pair))

    kv_block = paired(jnp.where(even, wk, wv), jnp.where(even, wv, wk))
    stream = Stream(
        qkvo=jnp.concatenate([shared_out(wq), kv_block, shared_out(wo)], 1),
        gu=jnp.concatenate([shared_out(wg), shared_out(wu)], 1),
        d=shared_out(wd),
    )

    q_at = tp_index * 2 * qcols + pair * qcols
    k_at = tp_index * kcols
    f_at = tp_index * 2 * fcols + pair * fcols
    q_scale = lax.dynamic_slice_in_dim(query_scale, q_at, qcols, 0)
    k_scale = lax.dynamic_slice_in_dim(key_scale, k_at, kcols, 0)
    v_scale = lax.dynamic_slice_in_dim(value_scale, k_at, kcols, 0)
    kv_scale = jnp.where(even, k_scale, v_scale)
    g_scale = lax.dynamic_slice_in_dim(gate_scale, f_at, fcols, 0)
    u_scale = lax.dynamic_slice_in_dim(up_scale, f_at, fcols, 0)

    inputs = tokens.astype(jnp.float32)
    inverse_one = inverse_rms(inputs)
    h_local = (inputs * inverse_one * pre_attention).astype(jnp.bfloat16)
    h_local = stream.stop(h_local, start=[("w_qkvo", ["qkvo"], over_line)])
    h_one = gather8(h_local)
    h_one = stream.stop(h_one, ["w_qkvo"], [("w_gu", ["gu"], over_line)])
    w_qkv = stream.blocks["w_qkvo"][:, : qcols + kcols]
    w_o = stream.blocks["w_qkvo"][:, qcols + kcols :]
    places = in_order(positions, swapped(positions, "pair"), pair)
    cosine, sine = phases(places)

    z_qkv = jnp.dot(h_one, w_qkv, preferred_element_type=jnp.float32)
    z_qkv = to_tokens(z_qkv, pair, row, core)
    zq, zkv = z_qkv[:, :qcols], z_qkv[:, qcols:]
    kv_rows = zkv * kv_scale
    kv_rows = jnp.where(even, rotate(kv_rows, cosine, sine), kv_rows).astype(jnp.bfloat16)
    depth = min((WINDOW - 1 + rows - 1) // rows, lines - 1)
    kept, other = [kv_rows], [swapped(kv_rows, "pair")]
    for step in range(depth):
        kept.append(hop(kept[-1], 1, step))
        kept[-1], other = stream.stop((kept[-1], other))
        other.append(swapped(kept[-1], "pair"))
    queries = (rotate(zq * q_scale, cosine, sine).astype(jnp.bfloat16) * scale).astype(jnp.bfloat16)
    kept, other = jnp.concatenate(kept[::-1], 0), jnp.concatenate(other[::-1], 0)
    keys = jnp.where(even, kept, other)
    values = jnp.where(even, other, kept)
    low = depth * rows + jnp.arange(rows, dtype=jnp.int32) - jnp.minimum(places, WINDOW - 1)
    low = low[:, None]
    attended_wide, lse = attend(queries, keys, values, low)
    attended = attended_wide.astype(jnp.bfloat16)
    attended = from_tokens(attended, pair, row, core)
    def by_core(left, right):
        half_rows = left.shape[0] // 2
        mine, others = left[:half_rows], left[half_rows:]
        others = jnp.einsum("tc,dc->td", others, right, preferred_element_type=jnp.float32)
        mine, others = tie(mine, others.astype(jnp.bfloat16))
        mine = jnp.einsum("tc,dc->td", mine, right, preferred_element_type=jnp.float32)
        return mine, others

    zo = scatter8(by_core(attended, w_o))
    zo = stream.stop(zo, ["w_gu"], [("w_d", ["d"], over_line)])
    w_gu, w_d = stream.blocks["w_gu"], stream.blocks["w_d"]
    after_attention = zo * output_scale
    inverse_two = inverse_rms(after_attention)
    middle = inputs + after_attention * inverse_two * post_attention
    inverse_three = inverse_rms(middle)
    h_two = gather8((middle * inverse_three * pre_feedforward).astype(jnp.bfloat16))
    z_gu = jnp.dot(h_two, w_gu, preferred_element_type=jnp.float32)
    zg, zu = z_gu[:, :fcols], z_gu[:, fcols:]
    gate_in = zg * g_scale
    up_in = zu * u_scale
    hidden = (jax.nn.gelu(gate_in, approximate=True) * up_in).astype(jnp.bfloat16)
    zd = scatter8(by_core(hidden, w_d))
    fed = zd * down_scale
    inverse_four = inverse_rms(fed)
    block_out = middle + fed * inverse_four * post_feedforward

    upstream = cotangent.astype(jnp.float32)
    dfed, gain_four_grad = norm_back(fed, inverse_four, post_feedforward, upstream)
    down_scale_sum = jnp.sum(dfed * zd, axis=0)
    def over_line_sum(term):
        return lax.psum_scatter(term, "line", scatter_dimension=0, tiled=True)

    def rows_for(part, place):
        size = part.shape[0] // 2
        return lax.dynamic_slice_in_dim(part, place * size, size, 0).astype(jnp.float32)

    def swap_of(name):
        def route(part):
            return swapped(rows_for(part, 1 - pair).astype(jnp.bfloat16), "pair")

        return (name + "_got", [name + "_sum"], route)

    def shared(name):
        return rows_for(stream.blocks[name + "_sum"], pair), stream.blocks[name + "_got"].astype(
            jnp.float32
        )

    def side_by_side(keep, got, first):
        return jnp.where(
            first, jnp.concatenate([keep, got], 1), jnp.concatenate([got, keep], 1)
        )

    def term_of(left, right):
        return jnp.einsum("td,tf->df", left, right, preferred_element_type=jnp.float32).astype(
            jnp.bfloat16
        )

    def down_term(four, other):
        mine = jnp.einsum("td,tf->df", four, hidden[: rows // 2], preferred_element_type=jnp.float32)
        mine, other = tie(mine, other)
        others = jnp.einsum(
            "td,tf->df", other, hidden[rows // 2 :], preferred_element_type=jnp.float32
        )
        stream.blocks["D"] = (mine + others).astype(jnp.bfloat16)
        return stream.stop((four, other), ["D"], [("D_sum", ["D"], over_line_sum)])

    dzd = gather8((dfed * down_scale).astype(jnp.bfloat16), down_term)
    dhidden = jnp.dot(dzd, w_d, preferred_element_type=jnp.float32)
    unused, pull = jax.vjp(
        lambda left, right: jax.nn.gelu(left, approximate=True) * right, gate_in, up_in
    )
    dgate, dup = pull(dhidden)
    gate_scale_sum = jnp.sum(dgate * zg, axis=0)
    up_scale_sum = jnp.sum(dup * zu, axis=0)
    dzg = (dgate * g_scale).astype(jnp.bfloat16)
    dzu = (dup * u_scale).astype(jnp.bfloat16)
    dh_mid = (
        jnp.einsum("tf,df->td", dzg, w_gu[:, :fcols], preferred_element_type=jnp.float32)
        + jnp.einsum("tf,df->td", dzu, w_gu[:, fcols:], preferred_element_type=jnp.float32)
    )
    stream.blocks["GU"] = jnp.concatenate([term_of(h_two, dzg), term_of(h_two, dzu)], 1)
    dh_mid = scatter8(
        jnp.split(dh_mid, 2),
        lambda work: stream.stop(
            work, ["GU", "D_sum"], [("GU_sum", ["GU"], over_line_sum), swap_of("D")]
        ),
    )
    dmid_norm, gain_three_grad = norm_back(middle, inverse_three, pre_feedforward, dh_mid)
    dmiddle = upstream + dmid_norm
    dafter, gain_two_grad = norm_back(after_attention, inverse_two, post_attention, dmiddle)
    output_scale_sum = jnp.sum(dafter * zo, axis=0)
    early = (
        output_scale_sum,
        spread(gate_scale_sum, gate_scale.shape[0], f_at),
        spread(up_scale_sum, up_scale.shape[0], f_at),
        down_scale_sum,
        gain_two_grad,
        gain_three_grad,
        gain_four_grad,
    )
    dzo = gather8((dafter * output_scale).astype(jnp.bfloat16), direct=True)
    o_term = term_of(dzo, attended)
    dattended = jnp.dot(dzo, w_o, preferred_element_type=jnp.float32).astype(jnp.bfloat16)
    dattended = to_tokens(dattended, pair, row, core)
    delta = jnp.sum(dattended.astype(jnp.float32) * attended_wide, axis=-1, keepdims=True)
    dqueries, dkeys, dvalues = attend_back(queries, keys, values, low, lse, delta, dattended)
    dqueries = dqueries.T * scale

    keep = jnp.where(even, dkeys, dvalues)
    give = jnp.where(even, dvalues, dkeys).astype(jnp.bfloat16)
    got = [swapped(give[i * rows : (i + 1) * rows], "pair") for i in range(depth + 1)]
    equery = rotate(dqueries, cosine, -sine)
    query_scale_sum = jnp.sum(equery * zq, axis=0)
    dzq = from_tokens((equery * q_scale).astype(jnp.bfloat16), pair, row, core)
    q_term = term_of(h_one, dzq)
    got[0], q_term, o_term = stream.stop((got[0], q_term, o_term))
    dkv = None
    for i in range(depth + 1):
        block = keep[i * rows : (i + 1) * rows] + got[i].astype(jnp.float32)
        if dkv is not None:
            block = block + hop(dkv.astype(jnp.bfloat16), -1, depth + 1 - i).astype(jnp.float32)
        dkv = block
    ekv = jnp.where(even, rotate(dkv, cosine, -sine), dkv)
    kv_scale_sum = jnp.sum(ekv * zkv, axis=0)
    dzkv = from_tokens((ekv * kv_scale).astype(jnp.bfloat16), pair, row, core)
    kv_term = term_of(h_one, dzkv)
    stream.blocks["QKVO"] = jnp.concatenate([q_term, kv_term, o_term], 1)
    dzkv = stream.stop(
        dzkv,
        ["QKVO", "GU_sum", "D_got"],
        [("QKVO_sum", ["QKVO"], over_line_sum), swap_of("GU")],
    )
    dh_one = jnp.einsum(
        "tc,dc->td",
        jnp.concatenate([dzq, dzkv], 1),
        w_qkv,
        preferred_element_type=jnp.float32,
    )
    gain_one_part = jnp.sum(dh_one * h_one.astype(jnp.float32), axis=0) / pre_attention
    late = (
        spread(query_scale_sum, query_scale.shape[0], q_at),
        spread(jnp.where(even, kv_scale_sum, 0.0), key_scale.shape[0], k_at),
        spread(jnp.where(even, 0.0, kv_scale_sum), value_scale.shape[0], k_at),
        gain_one_part,
    )
    sums = jnp.concatenate(early + late)
    dh_one, sums = stream.stop((dh_one, sums), ["GU_got"])
    for axis in ["core", "row", "pair"] + [1 << i for i in range(lines.bit_length() - 1)]:
        sums = sums + exchanged(sums, axis)
    stream.blocks["sums"] = sums
    dh_local = scatter8_last(
        jnp.split(dh_one, 2),
        lambda work: stream.stop(work, ["QKVO_sum", "sums"], [swap_of("QKVO")]),
    )
    sums = stream.blocks["sums"]
    dinput_norm, unused = norm_back(inputs, inverse_one, pre_attention, dh_local)
    token_grad = dmiddle + dinput_norm
    d_keep, d_got = shared("D")
    down_grad = side_by_side(d_keep, d_got, even).T
    gu_keep, gu_got = shared("GU")
    gate_grad = side_by_side(gu_keep[:, :fcols], gu_got[:, :fcols], even)
    up_grad = side_by_side(gu_keep[:, fcols:], gu_got[:, fcols:], even)
    keep, got = shared("QKVO")
    query_grad = side_by_side(keep[:, :qcols], got[:, :qcols], even)
    kv_keep, kv_got = keep[:, qcols : qcols + kcols], got[:, qcols : qcols + kcols]
    key_grad = jnp.where(even, kv_keep, kv_got)
    value_grad = jnp.where(even, kv_got, kv_keep)
    output_grad = side_by_side(keep[:, qcols + kcols :], got[:, qcols + kcols :], even).T

    cuts, at = [], 0
    for vector in early + late:
        cuts.append(sums[at : at + vector.shape[0]])
        at += vector.shape[0]
    o_sum, g_sum, u_sum, d_sum, two_sum, three_sum, four_sum, q_sum, k_sum, v_sum, one_sum = cuts
    return (
        block_out,
        token_grad,
        query_grad,
        key_grad,
        value_grad,
        output_grad,
        gate_grad,
        up_grad,
        down_grad,
        q_sum,
        k_sum,
        v_sum,
        o_sum,
        g_sum,
        u_sum,
        d_sum,
        one_sum,
        two_sum,
        three_sum,
        four_sum,
    )


def solution(mesh):
    seq_count, tp_count = mesh.shape["seq"], mesh.shape["tp"]
    wide = Mesh(mesh.devices.reshape(seq_count // 2, 2, tp_count // 2, 2), EVERY)
    seq, tp = ("line", "pair"), ("row", "core")
    return jax.shard_map(
        body,
        mesh=wide,
        in_specs=(P(EVERY, None),) * 2
        + (P(seq, tp),) * 3
        + (P(tp, seq),)
        + (P(seq, tp),) * 2
        + (P(tp, seq),)
        + (P(),) * 11
        + (P(seq),),
        out_specs=(P(EVERY, None),) * 2
        + (P(seq, tp),) * 3
        + (P(tp, seq),)
        + (P(seq, tp),) * 2
        + (P(tp, seq),)
        + (P(),) * 11,
        check_vma=False,
    )
```

profile of v0, /device:TPU:0, one launch (start us, length us, event | category | flops | bytes accessed | tf_op | source)
XLA Modules:
  0.0 900.3 jit_solution(13048968690272725620)
XLA Ops:
  56.7 15.8 %collective-permute-done = s32[512]{0:T(512)S(1)} collective-permute-done((s32[512]{0:T(512)S(1)}, s32[512]{0:T(512)S(1)}, u32[]{:S(2)}, u32[]{:S(2)}) %collective-permute-start) | collective-permute-done | bytes 2080 | tf_op jit(solution)/shard_map/ppermute | solution.py:21
  84.2 10.5 %all-gather.4.cloned.1.call-done = bf16[2304,768]{1,0:T(8,128)(2,1)} async-done(((bf16[576,768]{1,0:T(8,128)(2,1)}), bf16[2304,768]{1,0:T(8,128)(2,1)}) %all-gather.4.cloned.1.call-update) | async-done | bytes 3538960 | tf_op jit(solution)/shard_map/all_gather | solution.py:366
  106.3 20.8 %collective-permute-done.13 = bf16[1024,256]{1,0:T(8,128)(2,1)S(1)} collective-permute-done((bf16[1024,256]{1,0:T(8,128)(2,1)S(1)}, bf16[1024,256]{1,0:T(8,128)(2,1)S(1)}, u32[]{:S(2)}, u32[]{:S(2)}) %collective-permute-start.13) | collective-permute-done | bytes 524320 | tf_op jit(solution)/shard_map/ppermute | solution.py:27
  129.8 10.1 %collective-permute-done.16 = bf16[1024,256]{1,0:T(8,128)(2,1)S(1)} collective-permute-done((bf16[1024,256]{1,0:T(8,128)(2,1)S(1)}, bf16[1024,256]{1,0:T(8,128)(2,1)S(1)}, u32[]{:S(2)}, u32[]{:S(2)}) %collective-permute-start.16) | collective-permute-done | bytes 524320 | tf_op jit(solution)/shard_map/ppermute | solution.py:21
  143.8 10.5 %collective-permute-done.18 = bf16[1024,256]{1,0:T(8,128)(2,1)} collective-permute-done((bf16[1024,256]{1,0:T(8,128)(2,1)}, bf16[1024,256]{1,0:T(8,128)(2,1)}, u32[]{:S(2)}, u32[]{:S(2)}) %collective-permute-start.18) | collective-permute-done | bytes 524320 | tf_op jit(solution)/shard_map/ppermute | solution.py:21
  195.5 9.1 %collective-permute-done.21 = bf16[2,128,1152]{2,1,0:T(8,128)(2,1)S(1)} collective-permute-done((bf16[2,128,1152]{2,1,0:T(8,128)(2,1)S(1)}, bf16[2,128,1152]{2,1,0:T(8,128)(2,1)S(1)}, u32[]{:S(2)}, u32[]{:S(2)}) %collective-permute-start.21) | collective-permute-done | bytes 589856 | tf_op jit(solution)/shard_map/ppermute | solution.py:21
  216.6 70.8 %all-gather.6.cloned.1.call-done = bf16[2304,2304]{1,0:T(8,128)(2,1)} async-done(((bf16[576,2304]{1,0:T(8,128)(2,1)}), bf16[2304,2304]{1,0:T(8,128)(2,1)}) %all-gather.6.cloned.1.call-update) | async-done | bytes 10616848 | tf_op jit(solution)/shard_map/all_gather | solution.py:366
  319.3 15.5 %fusion.132 = f32[1024,2304]{1,0:T(8,128)S(1)} fusion(bf16[1024,2304]{1,0:T(8,128)(2,1)S(1)} %shard_map.360, bf16[2304,2304]{1,0:T(8,128)(2,1)} %all-gather.6.cloned.1.call-done), kind=kOutput, calls=%fused_computation.378 | convolution fusion | flops 10871635968 | bytes 24772608 | tf_op jit(solution)/shard_map/dot_general | solution.py:435
  339.6 72.4 %all-gather.8.cloned.1.call-done = bf16[2304,1152]{1,0:T(8,128)(2,1)} async-done(((bf16[576,1152]{1,0:T(8,128)(2,1)}), bf16[2304,1152]{1,0:T(8,128)(2,1)}) %all-gather.8.cloned.1.call-update) | async-done | bytes 5308432 | tf_op jit(solution)/shard_map/all_gather | solution.py:366
  426.3 12.4 %collective-permute-done.34 = bf16[2,128,1152]{2,1,0:T(8,128)(2,1)S(1)} collective-permute-done((bf16[2,128,1152]{2,1,0:T(8,128)(2,1)S(1)}, bf16[2,128,1152]{2,1,0:T(8,128)(2,1)S(1)}, u32[]{:S(2)}, u32[]{:S(2)}) %collective-permute-start.34) | collective-permute-done | bytes 589856 | tf_op jit(solution)/shard_map/ppermute | solution.py:21
  487.7 16.7 %multiply_reduce_fusion.1 = (f32[1152]{0:T(1024)S(1)}, f32[1152]{0:T(1024)}, f32[1024,1152]{1,0:T(8,128)}, bf16[1024,1152]{1,0:T(8,128)(2,1)S(1)}) fusion(f32[1024,2304]{1,0:T(8,128)} %copy-done.38, f32[1152]{0:T(1024)S(1)} %dynamic_slice.240, f32[1152]{0:T(1024)S(1)} %dynamic_slice.241, bf16[1024,2304]{1,0:T(8,128)(2,1)S(1)} %shard_map.362, ...), kind=kOutput, calls=%fused_computation.23 | convolution fusion | flops 5471205376 | bytes 26560512 | tf_op jit(solution)/shard_map/dot_general | solution.py:486
  504.5 11.4 %fusion.1 = f32[1024,2304]{1,0:T(8,128)} fusion(bf16[2304,2304]{1,0:T(8,128)(2,1)S(1)} %bitcast.152, f32[1024,1152]{1,0:T(8,128)} %get-tuple-element.144, f32[1152]{0:T(1024)S(1)} %dynamic_slice.240), kind=kOutput, calls=%fused_computation.9 | convolution fusion | flops 5438177280 | bytes 19472384 | tf_op jit(solution)/shard_map/tf,df->td/dot_general | solution.py:496
  515.8 10.5 %convolution_add_fusion = f32[1024,2304]{1,0:T(8,128)S(1)} fusion(f32[1024,2304]{1,0:T(8,128)} %fusion.1, bf16[1024,1152]{1,0:T(8,128)(2,1)S(1)} %get-tuple-element.167, bf16[2304,2304]{1,0:T(8,128)(2,1)} %all-gather.6.cloned.1.call-done), kind=kOutput, calls=%fused_computation.7 | convolution fusion | flops 5438177280 | bytes 26542080 | tf_op jit(solution)/shard_map/tf,df->td/dot_general | solution.py:497
  555.3 22.3 %reduce-scatter.4.cloned.1.call-done = bf16[576,1152]{1,0:T(8,128)(2,1)} async-done(((bf16[2304,1152]{1,0:T(8,128)(2,1)}), bf16[576,1152]{1,0:T(8,128)(2,1)}) %reduce-scatter.4.cloned.1.call-update) | async-done | bytes 1327120 | tf_op jit(solution)/shard_map/reduce_scatter | solution.py:449
  583.4 12.2 %collective-permute-done.46 = bf16[2,128,1152]{2,1,0:T(8,128)(2,1)S(1)} collective-permute-done((bf16[2,128,1152]{2,1,0:T(8,128)(2,1)S(1)}, bf16[2,128,1152]{2,1,0:T(8,128)(2,1)S(1)}, u32[]{:S(2)}, u32[]{:S(2)}) %collective-permute-start.46) | collective-permute-done | bytes 589856 | tf_op jit(solution)/shard_map/ppermute | solution.py:21
  613.2 11.9 %collective-permute-done.50.refs_1_ = bf16[128,2304]{1,0:T(8,128)(2,1)S(1)} collective-permute-done((bf16[128,2304]{1,0:T(8,128)(2,1)S(1)}, bf16[128,2304]{1,0:T(8,128)(2,1)S(1)}, u32[]{:S(2)}, u32[]{:S(2)}) %collective-permute-start.50) | collective-permute-done | bytes 589856 | tf_op jit(solution)/shard_map/ppermute | solution.py:21
  626.6 9.9 %collective-permute-done.52.refs_3_ = bf16[128,2304]{1,0:T(8,128)(2,1)S(1)} collective-permute-done((bf16[128,2304]{1,0:T(8,128)(2,1)S(1)}, bf16[128,2304]{1,0:T(8,128)(2,1)S(1)}, u32[]{:S(2)}, u32[]{:S(2)}) %collective-permute-start.52) | collective-permute-done | bytes 589856 | tf_op jit(solution)/shard_map/ppermute | solution.py:136
  651.3 10.4 %shard_map.365 = (f32[256,1024]{1,0:T(8,128)S(1)}, f32[4096,256]{1,0:T(8,128)}, f32[4096,256]{1,0:T(8,128)}) custom-call(s32[1]{0:T(128)S(6)} %select_n.277.first_ref, bf16[1024,256]{1,0:T(8,128)(2,1)S(1)} %copy-done.11, bf16[1024,256]{1,0:T(8,128)(2,1)S(1)} %constant_dynamic-update-slice_fusion.4.up_ref, bf16[4096,256]{1,0:T(8,128)(2,1)S(1)} %copy-done.1, ...), custom_call_target="tpu_custom_call" | custom-call | flops 10737418240 | bytes 12582912 | tf_op jit(solution)/shard_map/pallas_call | solution.py:304
  682.2 9.7 %collective-permute-done.56 = bf16[1024,256]{1,0:T(8,128)(2,1)S(1)} collective-permute-done((bf16[1024,256]{1,0:T(8,128)(2,1)S(1)}, bf16[1024,256]{1,0:T(8,128)(2,1)S(1)}, u32[]{:S(2)}, u32[]{:S(2)}) %collective-permute-start.56) | collective-permute-done | bytes 524320 | tf_op jit(solution)/shard_map/ppermute | solution.py:21
  712.7 15.5 %collective-permute-done.54 = bf16[1024,256]{1,0:T(8,128)(2,1)S(1)} collective-permute-done((bf16[1024,256]{1,0:T(8,128)(2,1)}, bf16[1024,256]{1,0:T(8,128)(2,1)S(1)}, u32[]{:S(2)}, u32[]{:S(2)}) %collective-permute-start.54) | collective-permute-done | bytes 524320 | tf_op jit(solution)/shard_map/ppermute | solution.py:21
  728.3 40.0 %collective-permute-done.60 = bf16[1024,256]{1,0:T(8,128)(2,1)S(1)} collective-permute-done((bf16[1024,256]{1,0:T(8,128)(2,1)S(1)}, bf16[1024,256]{1,0:T(8,128)(2,1)S(1)}, u32[]{:S(2)}, u32[]{:S(2)}) %collective-permute-start.60) | collective-permute-done | bytes 524320 | tf_op jit(solution)/shard_map/ppermute | solution.py:27
  779.4 14.2 %reduce-scatter.6.cloned.1.call-done = bf16[576,2304]{1,0:T(8,128)(2,1)} async-done(((bf16[2304,2304]{1,0:T(8,128)(2,1)}), bf16[576,2304]{1,0:T(8,128)(2,1)}) %reduce-scatter.6.cloned.1.call-update) | async-done | bytes 2654224 | tf_op jit(solution)/shard_map/reduce_scatter | solution.py:449
  803.7 23.2 %collective-permute-done.62 = bf16[288,2304]{1,0:T(8,128)(2,1)S(1)} collective-permute-done((bf16[288,2304]{1,0:T(8,128)(2,1)}, bf16[288,2304]{1,0:T(8,128)(2,1)S(1)}, u32[]{:S(2)}, u32[]{:S(2)}) %collective-permute-start.62) | collective-permute-done | bytes 1327136 | tf_op jit(solution)/shard_map/ppermute | solution.py:21
  845.8 12.0 %collective-permute-done.68 = f32[36352]{0:T(1024)S(1)} collective-permute-done((f32[36352]{0:T(1024)S(1)}, f32[36352]{0:T(1024)S(1)}, u32[]{:S(2)}, u32[]{:S(2)}) %collective-permute-start.68) | collective-permute-done | bytes 145440 | tf_op jit(solution)/shard_map/ppermute | solution.py:224
  (575 shorter events, 413.1 us)
Async XLA Ops:
  7.2 87.5 %all-gather.4.cloned.1.call-start = ((), (), s32[]{:S(2)}) async-start(), calls=%async_computation.3 | async-start | bytes 4423680 | tf_op jit(solution)/shard_map/all_gather | solution.py:366
  23.1 264.3 %all-gather.6.cloned.1.call-start = ((), (), s32[]{:S(2)}) async-start(), calls=%async_computation.4 | async-start | bytes 13271040 | tf_op jit(solution)/shard_map/all_gather | solution.py:366
  42.0 31.3 %collective-permute-start.12 = (bf16[288,1152]{1,0:T(8,128)(2,1)}, bf16[288,1152]{1,0:T(8,128)(2,1)}, u32[]{:S(2)}, u32[]{:S(2)}) collective-permute-start(bf16[288,1152]{1,0:T(8,128)(2,1)} %get-tuple-element.196), channel_id=1, source_target_pairs={{0,4},{4,0},{1,5},{5,1},{2,6},{6,2},{3,7},{7,3},{8,12},{12,8},{9,1... | collective-permute-start | bytes 1990664 | tf_op jit(solution)/shard_map/ppermute | solution.py:21
  51.1 29.0 %collective-permute-start.10 = (bf16[512,2304]{1,0:T(8,128)(2,1)S(1)}, bf16[512,2304]{1,0:T(8,128)(2,1)}, u32[]{:S(2)}, u32[]{:S(2)}) collective-permute-start(bf16[512,2304]{1,0:T(8,128)(2,1)S(1)} %shard_map.356.refs_0_), channel_id=1, source_target_pairs={{0,1},{1,0},{2,3},{3,2},{4,5},{5,4},{6,7},{7,6},{8,9},{9,8},{10,11... | collective-permute-start | bytes 7077896 | tf_op jit(solution)/shard_map/ppermute | solution.py:21
  53.0 22.8 %collective-permute-start.11 = (bf16[288,1152]{1,0:T(8,128)(2,1)}, bf16[288,1152]{1,0:T(8,128)(2,1)}, u32[]{:S(2)}, u32[]{:S(2)}) collective-permute-start(bf16[288,1152]{1,0:T(8,128)(2,1)} %get-tuple-element.194), channel_id=1, source_target_pairs={{0,4},{4,0},{1,5},{5,1},{2,6},{6,2},{3,7},{7,3},{8,12},{12,8},{9,1... | collective-permute-start | bytes 1990664 | tf_op jit(solution)/shard_map/ppermute | solution.py:21
  54.6 18.0 %collective-permute-start = (s32[512]{0:T(512)S(1)}, s32[512]{0:T(512)S(1)}, u32[]{:S(2)}, u32[]{:S(2)}) collective-permute-start(s32[512]{0:T(512)S(1)} %copy-done.82), channel_id=1, source_target_pairs={{0,4},{4,0},{1,5},{5,1},{2,6},{6,2},{3,7},{7,3},{8,12},{12,8},{9,1... | collective-permute-start | bytes 6152 | tf_op jit(solution)/shard_map/ppermute | solution.py:21
  94.8 317.2 %all-gather.8.cloned.1.call-start = ((), (), s32[]{:S(2)}) async-start(), calls=%async_computation.5 | async-start | bytes 6635520 | tf_op jit(solution)/shard_map/all_gather | solution.py:366
  103.5 23.6 %collective-permute-start.13 = (bf16[1024,256]{1,0:T(8,128)(2,1)S(1)}, bf16[1024,256]{1,0:T(8,128)(2,1)S(1)}, u32[]{:S(2)}, u32[]{:S(2)}) collective-permute-start(bf16[1024,256]{1,0:T(8,128)(2,1)S(1)} %fusion.46), channel_id=1, source_target_pairs={{0,8},{8,16},{16,24},{1,9},{9,17},{17,25},{2,10},{10,18},{18,26},{... | collective-permute-start | bytes 1572872 | tf_op jit(solution)/shard_map/ppermute | solution.py:27
  104.8 22.3 %collective-permute-start.14 = (bf16[1024,256]{1,0:T(8,128)(2,1)S(1)}, bf16[1024,256]{1,0:T(8,128)(2,1)S(1)}, u32[]{:S(2)}, u32[]{:S(2)}) collective-permute-start(bf16[1024,256]{1,0:T(8,128)(2,1)S(1)} %fusion.46), channel_id=1, source_target_pairs={{0,4},{4,0},{1,5},{5,1},{2,6},{6,2},{3,7},{7,3},{8,12},{12,8},{9,1... | collective-permute-start | bytes 1572872 | tf_op jit(solution)/shard_map/ppermute | solution.py:21
  174.6 17.8 %collective-permute-start.25 = (bf16[288,1152]{1,0:T(8,128)(2,1)S(1)}, bf16[288,1152]{1,0:T(8,128)(2,1)S(1)}, u32[]{:S(2)}, u32[]{:S(2)}) collective-permute-start(bf16[288,1152]{1,0:T(8,128)(2,1)S(1)} %get-tuple-element.192), channel_id=1, source_target_pairs={{0,4},{4,0},{1,5},{5,1},{2,6},{6,2},{3,7},{7,3},{8,12},{12,8},{9,1... | collective-permute-start | bytes 1990664 | tf_op jit(solution)/shard_map/ppermute | solution.py:21
  181.3 23.4 %collective-permute-start.21 = (bf16[2,128,1152]{2,1,0:T(8,128)(2,1)S(1)}, bf16[2,128,1152]{2,1,0:T(8,128)(2,1)S(1)}, u32[]{:S(2)}, u32[]{:S(2)}) collective-permute-start(bf16[2,128,1152]{2,1,0:T(8,128)(2,1)S(1)} %slice_bitcast_fusion.17), channel_id=1, source_target_pairs={{0,4},{4,0},{1,5},{5,1},{2,6},{6,2},{3,7},{7,3},{8,12},{12,8},{9,1... | collective-permute-start | bytes 1769480 | tf_op jit(solution)/shard_map/ppermute | solution.py:21
  182.6 22.0 %collective-permute-start.23 = (bf16[2,128,1152]{2,1,0:T(8,128)(2,1)S(1)}, bf16[2,128,1152]{2,1,0:T(8,128)(2,1)S(1)}, u32[]{:S(2)}, u32[]{:S(2)}) collective-permute-start(bf16[2,128,1152]{2,1,0:T(8,128)(2,1)S(1)} %slice_bitcast_fusion.15), channel_id=1, source_target_pairs={{0,2},{2,0},{1,3},{3,1},{4,6},{6,4},{5,7},{7,5},{8,10},{10,8},{9,1... | collective-permute-start | bytes 1769480 | tf_op jit(solution)/shard_map/ppermute | solution.py:21
  288.8 288.8 %reduce-scatter.4.cloned.1.call-start = ((), (), s32[]{:S(2)}) async-start(), calls=%async_computation.6 | async-start | bytes 6635520 | tf_op jit(solution)/shard_map/reduce_scatter | solution.py:449
  485.2 308.3 %reduce-scatter.6.cloned.1.call-start = ((), (), s32[]{:S(2)}) async-start(), calls=%async_computation.7 | async-start | bytes 13271040 | tf_op jit(solution)/shard_map/reduce_scatter | solution.py:449
  526.6 22.9 %collective-permute-start.45 = (bf16[512,2304]{1,0:T(8,128)(2,1)S(1)}, bf16[512,2304]{1,0:T(8,128)(2,1)}, u32[]{:S(2)}, u32[]{:S(2)}) collective-permute-start(bf16[512,2304]{1,0:T(8,128)(2,1)S(1)} %split.25), channel_id=1, source_target_pairs={{0,1},{1,0},{2,3},{3,2},{4,5},{5,4},{6,7},{7,6},{8,9},{9,8},{10,11... | collective-permute-start | bytes 7077896 | tf_op jit(solution)/shard_map/ppermute | solution.py:21
  579.0 291.9 %reduce-scatter.8.cloned.1.call-start = ((), (), s32[]{:S(2)}) async-start(), calls=%async_computation.8 | async-start | bytes 4423680 | tf_op jit(solution)/shard_map/reduce_scatter | solution.py:449
  610.9 25.6 %collective-permute-start.52 = (bf16[128,2304]{1,0:T(8,128)(2,1)S(1)}, bf16[128,2304]{1,0:T(8,128)(2,1)S(1)}, u32[]{:S(2)}, u32[]{:S(2)}) collective-permute-start(bf16[128,2304]{1,0:T(8,128)(2,1)S(1)} %get-tuple-element.178.refs_0_), channel_id=1, source_target_pairs={{0,6},{2,4},{4,2},{6,0},{1,7},{3,5},{5,3},{7,1},{8,14},{10,12},{12... | collective-permute-start | bytes 1769480 | tf_op jit(solution)/shard_map/ppermute | solution.py:136
  672.5 19.5 %collective-permute-start.56 = (bf16[1024,256]{1,0:T(8,128)(2,1)S(1)}, bf16[1024,256]{1,0:T(8,128)(2,1)S(1)}, u32[]{:S(2)}, u32[]{:S(2)}) collective-permute-start(bf16[1024,256]{1,0:T(8,128)(2,1)S(1)} %get-tuple-element.182), channel_id=1, source_target_pairs={{0,4},{4,0},{1,5},{5,1},{2,6},{6,2},{3,7},{7,3},{8,12},{12,8},{9,1... | collective-permute-start | bytes 1572872 | tf_op jit(solution)/shard_map/ppermute | solution.py:21
  681.6 21.6 %collective-permute-start.55 = (bf16[1024,256]{1,0:T(8,128)(2,1)}, bf16[1024,256]{1,0:T(8,128)(2,1)S(1)}, u32[]{:S(2)}, u32[]{:S(2)}) collective-permute-start(bf16[1024,256]{1,0:T(8,128)(2,1)} %get-tuple-element.183), channel_id=1, source_target_pairs={{0,4},{4,0},{1,5},{5,1},{2,6},{6,2},{3,7},{7,3},{8,12},{12,8},{9,1... | collective-permute-start | bytes 1572872 | tf_op jit(solution)/shard_map/ppermute | solution.py:21
  695.2 84.2 %collective-permute-start.61 = (bf16[288,1152]{1,0:T(8,128)(2,1)}, bf16[288,1152]{1,0:T(8,128)(2,1)}, u32[]{:S(2)}, u32[]{:S(2)}) collective-permute-start(bf16[288,1152]{1,0:T(8,128)(2,1)} %constant_dynamic-slice_fusion.2), channel_id=1, source_target_pairs={{0,4},{4,0},{1,5},{5,1},{2,6},{6,2},{3,7},{7,3},{8,12},{12,8},{9,1... | collective-permute-start | bytes 1990664 | tf_op jit(solution)/shard_map/ppermute | solution.py:21
  698.5 29.8 %collective-permute-start.54 = (bf16[1024,256]{1,0:T(8,128)(2,1)}, bf16[1024,256]{1,0:T(8,128)(2,1)S(1)}, u32[]{:S(2)}, u32[]{:S(2)}) collective-permute-start(bf16[1024,256]{1,0:T(8,128)(2,1)} %get-tuple-element.180), channel_id=1, source_target_pairs={{0,4},{4,0},{1,5},{5,1},{2,6},{6,2},{3,7},{7,3},{8,12},{12,8},{9,1... | collective-permute-start | bytes 1572872 | tf_op jit(solution)/shard_map/ppermute | solution.py:21
  704.7 63.5 %collective-permute-start.60 = (bf16[1024,256]{1,0:T(8,128)(2,1)S(1)}, bf16[1024,256]{1,0:T(8,128)(2,1)S(1)}, u32[]{:S(2)}, u32[]{:S(2)}) collective-permute-start(bf16[1024,256]{1,0:T(8,128)(2,1)S(1)} %fusion.44), channel_id=1, source_target_pairs={{8,0},{16,8},{24,16},{9,1},{17,9},{25,17},{10,2},{18,10},{26,18},{... | collective-permute-start | bytes 1572872 | tf_op jit(solution)/shard_map/ppermute | solution.py:27
  796.0 30.9 %collective-permute-start.62 = (bf16[288,2304]{1,0:T(8,128)(2,1)}, bf16[288,2304]{1,0:T(8,128)(2,1)S(1)}, u32[]{:S(2)}, u32[]{:S(2)}) collective-permute-start(bf16[288,2304]{1,0:T(8,128)(2,1)} %constant_dynamic-slice_fusion.1), channel_id=1, source_target_pairs={{0,4},{4,0},{1,5},{5,1},{2,6},{6,2},{3,7},{7,3},{8,12},{12,8},{9,1... | collective-permute-start | bytes 3981320 | tf_op jit(solution)/shard_map/ppermute | solution.py:21
  843.1 27.4 %collective-permute-start.64 = (bf16[2,128,2304]{2,1,0:T(8,128)(2,1)S(1)}, bf16[2,128,2304]{2,1,0:T(8,128)(2,1)S(1)}, u32[]{:S(2)}, u32[]{:S(2)}) collective-permute-start(bf16[2,128,2304]{2,1,0:T(8,128)(2,1)S(1)} %bitcast.150), channel_id=1, source_target_pairs={{0,4},{4,0},{1,5},{5,1},{2,6},{6,2},{3,7},{7,3},{8,12},{12,8},{9,1... | collective-permute-start | bytes 3538952 | tf_op jit(solution)/shard_map/ppermute | solution.py:21
  (154 other events, 2010.4 us)
Sparse Core Ops, SparseCore 0:
  23.2 71.4 all-gather.3
  96.9 190.4 all-gather.5
  289.0 122.8 all-gather.7
  485.4 92.1 reduce-scatter.3
  579.9 213.5 reduce-scatter.5
  797.6 73.1 reduce-scatter.7
where the time goes:
time: 910 us; the launch traced here: 900 us
  waiting for transfers between devices  522 us (57%)
  matrix products  109 us (12%)
  other arithmetic  85.5 us (9%)
  starting transfers between devices  78.5 us (9%)
  local copies, waits for them, and re-layouts  63.7 us (7%)
  Pallas kernels  22.2 us (2%)
  between operations  19.4 us (2%)
    ppermute x63, waiting for transfers between devices, swapped(): return lax.ppermute(block, axis, SWAP)  240 us
    all_gather x3, waiting for transfers between devices, over_line(): return lax.all_gather(block, 'line', axis=0, tiled=True)  154 us
    ppermute x63, starting transfers between devices, swapped(): return lax.ppermute(block, axis, SWAP)  66 us
    ppermute x6, waiting for transfers between devices, hop(): return lax.ppermute(block, 'line', route)  60.8 us
    reduce_scatter x3, waiting for transfers between devices, over_line_sum(): return lax.psum_scatter(term, 'line', scatter_dimension=0, tiled=True)  36.6 us
    unnamed x248, local copies, waits for them, and re-layouts  34.2 us
    dot_general x5, matrix products, term_of(): jnp.einsum('td,tf->df', left, right, preferred_element_type=jnp.float32)  22.7 us
    ppermute x2, waiting for transfers between devices, exchanged(): return lax.ppermute(vector, 'line', [(i, i ^ axis) for i in range(count)])  20.2 us
  transfers between devices with their start and end apart: 78, of which 53 were waited for; matrix products, arithmetic and copies ran while one was open for 23% of the time, Pallas kernels for 2%

commit v1 on v0

--- a/solution.py
+++ b/solution.py
@@ -182,11 +182,11 @@
     return jnp.concatenate([left, right], 1)
 
 
-def scatter8_last(terms, stop):
+def scatter8_last(terms, stop_one, stop_two):
     mine, others = terms
     size, width = mine.shape[0] // 4, mine.shape[1]
-    four = summed(mine, sent(others, "core")).reshape(2, 2, size, width)
-    two = stop(summed(four[0], sent(four[1], "pair")))
+    four = stop_one(summed(mine, sent(others, "core"))).reshape(2, 2, size, width)
+    two = stop_two(summed(four[0], sent(four[1], "pair")))
     return summed(two[0], sent(two[1], "row"))
 
 
@@ -475,11 +475,11 @@
 
     def down_term(four, other):
         mine = jnp.einsum("td,tf->df", four, hidden[: rows // 2], preferred_element_type=jnp.float32)
-        mine, other = tie(mine, other)
+        mine, other = tie(mine.astype(jnp.bfloat16), other)
         others = jnp.einsum(
             "td,tf->df", other, hidden[rows // 2 :], preferred_element_type=jnp.float32
         )
-        stream.blocks["D"] = (mine + others).astype(jnp.bfloat16)
+        stream.blocks["D"] = (mine.astype(jnp.float32) + others).astype(jnp.bfloat16)
         return stream.stop((four, other), ["D"], [("D_sum", ["D"], over_line_sum)])
 
     dzd = gather8((dfed * down_scale).astype(jnp.bfloat16), down_term)
@@ -562,22 +562,35 @@
         gain_one_part,
     )
     sums = jnp.concatenate(early + late)
-    dh_one, sums = stream.stop((dh_one, sums), ["GU_got"])
-    for axis in ["core", "row", "pair"] + [1 << i for i in range(lines.bit_length() - 1)]:
-        sums = sums + exchanged(sums, axis)
-    stream.blocks["sums"] = sums
-    dh_local = scatter8_last(
-        jnp.split(dh_one, 2),
-        lambda work: stream.stop(work, ["QKVO_sum", "sums"], [swap_of("QKVO")]),
-    )
-    sums = stream.blocks["sums"]
-    dinput_norm, unused = norm_back(inputs, inverse_one, pre_attention, dh_local)
-    token_grad = dmiddle + dinput_norm
+    stream.blocks["sums"] = sums + exchanged(sums, "pair")
+    dh_one = stream.stop(dh_one, ["GU_got", "sums"])
+    sum_axes = ["core", "row"] + [1 << i for i in range(lines.bit_length() - 1)]
     d_keep, d_got = shared("D")
     down_grad = side_by_side(d_keep, d_got, even).T
     gu_keep, gu_got = shared("GU")
     gate_grad = side_by_side(gu_keep[:, :fcols], gu_got[:, :fcols], even)
     up_grad = side_by_side(gu_keep[:, fcols:], gu_got[:, fcols:], even)
+    stream.blocks.update(gate=gate_grad, up=up_grad, down=down_grad)
+
+    def sums_after(four):
+        four = stream.stop(four, ["sums"])
+        for axis in sum_axes[:3]:
+            stream.blocks["sums"] += exchanged(stream.blocks["sums"], axis)
+        return four
+
+    dh_local = scatter8_last(
+        jnp.split(dh_one, 2),
+        sums_after,
+        lambda work: stream.stop(
+            work, ["QKVO_sum", "sums", "gate", "up", "down"], [swap_of("QKVO")]
+        ),
+    )
+    sums = stream.blocks["sums"]
+    for axis in sum_axes[3:]:
+        sums = sums + exchanged(sums, axis)
+    dinput_norm, unused = norm_back(inputs, inverse_one, pre_attention, dh_local)
+    token_grad = dmiddle + dinput_norm
+    gate_grad, up_grad, down_grad = (stream.blocks[name] for name in ("gate", "up", "down"))
     keep, got = shared("QKVO")
     query_grad = side_by_side(keep[:, :qcols], got[:, :qcols], even)
     kv_keep, kv_got = keep[:, qcols : qcols + kcols], got[:, qcols : qcols + kcols]

time: 910 us -> 905 us (level)
    unnamed x248 -> x252, local copies, waits for them, and re-layouts: 34.2 us -> 34.5 us
where the time goes in v1:
time: 905 us; the launch traced here: 896 us
  waiting for transfers between devices  517 us (57%)
  matrix products  112 us (12%)
  starting transfers between devices  81.3 us (9%)
  other arithmetic  80.7 us (9%)
  local copies, waits for them, and re-layouts  64.1 us (7%)
  Pallas kernels  21.7 us (2%)
  between operations  19.2 us (2%)
    ppermute x63, waiting for transfers between devices, swapped(): return lax.ppermute(block, axis, SWAP)  245 us
    all_gather x3, waiting for transfers between devices, over_line(): return lax.all_gather(block, 'line', axis=0, tiled=True)  154 us
    ppermute x63, starting transfers between devices, swapped(): return lax.ppermute(block, axis, SWAP)  66.2 us
    ppermute x6, waiting for transfers between devices, hop(): return lax.ppermute(block, 'line', route)  60.4 us
    reduce_scatter x3, waiting for transfers between devices, over_line_sum(): return lax.psum_scatter(term, 'line', scatter_dimension=0, tiled=True)  37.1 us
    unnamed x252, local copies, waits for them, and re-layouts  34.5 us
    dot_general x5, matrix products, term_of(): jnp.einsum('td,tf->df', left, right, preferred_element_type=jnp.float32)  22.8 us
  transfers between devices with their start and end apart: 78, of which 53 were waited for; matrix products, arithmetic and copies ran while one was open for 23% of the time, Pallas kernels for 2%

profile of v1, /device:TPU:0, one launch (start us, length us, event | category | flops | bytes accessed | tf_op | source)
XLA Modules:
  0.0 896.0 jit_solution(5963351570784956227)
XLA Ops:
  56.7 15.8 %collective-permute-done = s32[512]{0:T(512)S(1)} collective-permute-done((s32[512]{0:T(512)S(1)}, s32[512]{0:T(512)S(1)}, u32[]{:S(2)}, u32[]{:S(2)}) %collective-permute-start) | collective-permute-done | bytes 2080 | tf_op jit(solution)/shard_map/ppermute | solution.py:21
  84.2 10.5 %all-gather.4.cloned.1.call-done = bf16[2304,768]{1,0:T(8,128)(2,1)} async-done(((bf16[576,768]{1,0:T(8,128)(2,1)}), bf16[2304,768]{1,0:T(8,128)(2,1)}) %all-gather.4.cloned.1.call-update) | async-done | bytes 3538960 | tf_op jit(solution)/shard_map/all_gather | solution.py:366
  106.0 20.5 %collective-permute-done.13 = bf16[1024,256]{1,0:T(8,128)(2,1)S(1)} collective-permute-done((bf16[1024,256]{1,0:T(8,128)(2,1)S(1)}, bf16[1024,256]{1,0:T(8,128)(2,1)S(1)}, u32[]{:S(2)}, u32[]{:S(2)}) %collective-permute-start.13) | collective-permute-done | bytes 524320 | tf_op jit(solution)/shard_map/ppermute | solution.py:27
  129.3 10.0 %collective-permute-done.16 = bf16[1024,256]{1,0:T(8,128)(2,1)S(1)} collective-permute-done((bf16[1024,256]{1,0:T(8,128)(2,1)S(1)}, bf16[1024,256]{1,0:T(8,128)(2,1)S(1)}, u32[]{:S(2)}, u32[]{:S(2)}) %collective-permute-start.16) | collective-permute-done | bytes 524320 | tf_op jit(solution)/shard_map/ppermute | solution.py:21
  143.3 10.4 %collective-permute-done.18 = bf16[1024,256]{1,0:T(8,128)(2,1)} collective-permute-done((bf16[1024,256]{1,0:T(8,128)(2,1)}, bf16[1024,256]{1,0:T(8,128)(2,1)}, u32[]{:S(2)}, u32[]{:S(2)}) %collective-permute-start.18) | collective-permute-done | bytes 524320 | tf_op jit(solution)/shard_map/ppermute | solution.py:21
  195.0 9.1 %collective-permute-done.21 = bf16[2,128,1152]{2,1,0:T(8,128)(2,1)S(1)} collective-permute-done((bf16[2,128,1152]{2,1,0:T(8,128)(2,1)S(1)}, bf16[2,128,1152]{2,1,0:T(8,128)(2,1)S(1)}, u32[]{:S(2)}, u32[]{:S(2)}) %collective-permute-start.21) | collective-permute-done | bytes 589856 | tf_op jit(solution)/shard_map/ppermute | solution.py:21
  216.1 71.0 %all-gather.6.cloned.1.call-done = bf16[2304,2304]{1,0:T(8,128)(2,1)} async-done(((bf16[576,2304]{1,0:T(8,128)(2,1)}), bf16[2304,2304]{1,0:T(8,128)(2,1)}) %all-gather.6.cloned.1.call-update) | async-done | bytes 10616848 | tf_op jit(solution)/shard_map/all_gather | solution.py:366
  319.3 15.5 %fusion.133 = f32[1024,2304]{1,0:T(8,128)S(1)} fusion(bf16[1024,2304]{1,0:T(8,128)(2,1)S(1)} %shard_map.360, bf16[2304,2304]{1,0:T(8,128)(2,1)} %all-gather.6.cloned.1.call-done), kind=kOutput, calls=%fused_computation.378 | convolution fusion | flops 10871635968 | bytes 24772608 | tf_op jit(solution)/shard_map/dot_general | solution.py:435
  339.7 72.0 %all-gather.8.cloned.1.call-done = bf16[2304,1152]{1,0:T(8,128)(2,1)} async-done(((bf16[576,1152]{1,0:T(8,128)(2,1)}), bf16[2304,1152]{1,0:T(8,128)(2,1)}) %all-gather.8.cloned.1.call-update) | async-done | bytes 5308432 | tf_op jit(solution)/shard_map/all_gather | solution.py:366
  426.0 12.4 %collective-permute-done.34 = bf16[2,128,1152]{2,1,0:T(8,128)(2,1)S(1)} collective-permute-done((bf16[2,128,1152]{2,1,0:T(8,128)(2,1)S(1)}, bf16[2,128,1152]{2,1,0:T(8,128)(2,1)S(1)}, u32[]{:S(2)}, u32[]{:S(2)}) %collective-permute-start.34) | collective-permute-done | bytes 589856 | tf_op jit(solution)/shard_map/ppermute | solution.py:21
  485.7 16.5 %multiply_reduce_fusion.1 = (f32[1152]{0:T(1024)S(1)}, f32[1152]{0:T(1024)}, f32[1024,1152]{1,0:T(8,128)}, bf16[1024,1152]{1,0:T(8,128)(2,1)S(1)}) fusion(f32[1024,2304]{1,0:T(8,128)} %copy-done.38, f32[1152]{0:T(1024)S(1)} %dynamic_slice.240, f32[1152]{0:T(1024)S(1)} %dynamic_slice.241, bf16[1024,2304]{1,0:T(8,128)(2,1)S(1)} %shard_map.362, ...), kind=kOutput, calls=%fused_computation.24 | convolution fusion | flops 5471205376 | bytes 26560512 | tf_op jit(solution)/shard_map/dot_general | solution.py:486
  502.2 11.3 %fusion.1 = f32[1024,2304]{1,0:T(8,128)} fusion(bf16[2304,2304]{1,0:T(8,128)(2,1)S(1)} %bitcast.152, f32[1024,1152]{1,0:T(8,128)} %get-tuple-element.154, f32[1152]{0:T(1024)S(1)} %dynamic_slice.240), kind=kOutput, calls=%fused_computation.10 | convolution fusion | flops 5438177280 | bytes 19472384 | tf_op jit(solution)/shard_map/tf,df->td/dot_general | solution.py:496
  513.6 10.5 %convolution_add_fusion = f32[1024,2304]{1,0:T(8,128)S(1)} fusion(f32[1024,2304]{1,0:T(8,128)} %fusion.1, bf16[1024,1152]{1,0:T(8,128)(2,1)S(1)} %get-tuple-element.177, bf16[2304,2304]{1,0:T(8,128)(2,1)} %all-gather.6.cloned.1.call-done), kind=kOutput, calls=%fused_computation.8 | convolution fusion | flops 5438177280 | bytes 26542080 | tf_op jit(solution)/shard_map/tf,df->td/dot_general | solution.py:497
  553.3 22.6 %reduce-scatter.4.cloned.1.call-done = bf16[576,1152]{1,0:T(8,128)(2,1)} async-done(((bf16[2304,1152]{1,0:T(8,128)(2,1)}), bf16[576,1152]{1,0:T(8,128)(2,1)}) %reduce-scatter.4.cloned.1.call-update) | async-done | bytes 1327120 | tf_op jit(solution)/shard_map/reduce_scatter | solution.py:449
  581.7 12.2 %collective-permute-done.46 = bf16[2,128,1152]{2,1,0:T(8,128)(2,1)S(1)} collective-permute-done((bf16[2,128,1152]{2,1,0:T(8,128)(2,1)S(1)}, bf16[2,128,1152]{2,1,0:T(8,128)(2,1)S(1)}, u32[]{:S(2)}, u32[]{:S(2)}) %collective-permute-start.46) | collective-permute-done | bytes 589856 | tf_op jit(solution)/shard_map/ppermute | solution.py:21
  611.5 11.9 %collective-permute-done.50.refs_1_ = bf16[128,2304]{1,0:T(8,128)(2,1)S(1)} collective-permute-done((bf16[128,2304]{1,0:T(8,128)(2,1)S(1)}, bf16[128,2304]{1,0:T(8,128)(2,1)S(1)}, u32[]{:S(2)}, u32[]{:S(2)}) %collective-permute-start.50) | collective-permute-done | bytes 589856 | tf_op jit(solution)/shard_map/ppermute | solution.py:21
  624.9 9.9 %collective-permute-done.52.refs_3_ = bf16[128,2304]{1,0:T(8,128)(2,1)S(1)} collective-permute-done((bf16[128,2304]{1,0:T(8,128)(2,1)S(1)}, bf16[128,2304]{1,0:T(8,128)(2,1)S(1)}, u32[]{:S(2)}, u32[]{:S(2)}) %collective-permute-start.52) | collective-permute-done | bytes 589856 | tf_op jit(solution)/shard_map/ppermute | solution.py:136
  649.6 10.4 %shard_map.365 = (f32[256,1024]{1,0:T(8,128)S(1)}, f32[4096,256]{1,0:T(8,128)}, f32[4096,256]{1,0:T(8,128)}) custom-call(s32[1]{0:T(128)S(6)} %select_n.277.first_ref, bf16[1024,256]{1,0:T(8,128)(2,1)S(1)} %copy-done.11, bf16[1024,256]{1,0:T(8,128)(2,1)S(1)} %constant_dynamic-update-slice_fusion.4.up_ref, bf16[4096,256]{1,0:T(8,128)(2,1)S(1)} %copy-done.1, ...), custom_call_target="tpu_custom_call" | custom-call | flops 10737418240 | bytes 12582912 | tf_op jit(solution)/shard_map/pallas_call | solution.py:304
  680.5 9.7 %collective-permute-done.56 = bf16[1024,256]{1,0:T(8,128)(2,1)S(1)} collective-permute-done((bf16[1024,256]{1,0:T(8,128)(2,1)S(1)}, bf16[1024,256]{1,0:T(8,128)(2,1)S(1)}, u32[]{:S(2)}, u32[]{:S(2)}) %collective-permute-start.56) | collective-permute-done | bytes 524320 | tf_op jit(solution)/shard_map/ppermute | solution.py:21
  711.0 15.5 %collective-permute-done.54 = bf16[1024,256]{1,0:T(8,128)(2,1)S(1)} collective-permute-done((bf16[1024,256]{1,0:T(8,128)(2,1)}, bf16[1024,256]{1,0:T(8,128)(2,1)S(1)}, u32[]{:S(2)}, u32[]{:S(2)}) %collective-permute-start.54) | collective-permute-done | bytes 524320 | tf_op jit(solution)/shard_map/ppermute | solution.py:21
  726.5 39.9 %collective-permute-done.60 = bf16[1024,256]{1,0:T(8,128)(2,1)S(1)} collective-permute-done((bf16[1024,256]{1,0:T(8,128)(2,1)S(1)}, bf16[1024,256]{1,0:T(8,128)(2,1)S(1)}, u32[]{:S(2)}, u32[]{:S(2)}) %collective-permute-start.60) | collective-permute-done | bytes 524320 | tf_op jit(solution)/shard_map/ppermute | solution.py:27
  777.4 14.5 %reduce-scatter.6.cloned.1.call-done = bf16[576,2304]{1,0:T(8,128)(2,1)} async-done(((bf16[2304,2304]{1,0:T(8,128)(2,1)}), bf16[576,2304]{1,0:T(8,128)(2,1)}) %reduce-scatter.6.cloned.1.call-update) | async-done | bytes 2654224 | tf_op jit(solution)/shard_map/reduce_scatter | solution.py:449
  802.6 25.8 %collective-permute-done.63 = f32[36352]{0:T(1024)S(1)} collective-permute-done((f32[36352]{0:T(1024)S(1)}, f32[36352]{0:T(1024)S(1)}, u32[]{:S(2)}, u32[]{:S(2)}) %collective-permute-start.63) | collective-permute-done | bytes 145440 | tf_op jit(solution)/shard_map/ppermute | solution.py:21
  849.8 10.5 %collective-permute-done.68 = f32[36352]{0:T(1024)S(1)} collective-permute-done((f32[36352]{0:T(1024)S(1)}, f32[36352]{0:T(1024)S(1)}, u32[]{:S(2)}, u32[]{:S(2)}) %collective-permute-start.68) | collective-permute-done | bytes 145440 | tf_op jit(solution)/shard_map/ppermute | solution.py:224
  (579 shorter events, 408.1 us)
Async XLA Ops:
  7.2 87.5 %all-gather.4.cloned.1.call-start = ((), (), s32[]{:S(2)}) async-start(), calls=%async_computation.3 | async-start | bytes 4423680 | tf_op jit(solution)/shard_map/all_gather | solution.py:366
  23.1 264.0 %all-gather.6.cloned.1.call-start = ((), (), s32[]{:S(2)}) async-start(), calls=%async_computation.4 | async-start | bytes 13271040 | tf_op jit(solution)/shard_map/all_gather | solution.py:366
  42.0 31.3 %collective-permute-start.12 = (bf16[288,1152]{1,0:T(8,128)(2,1)}, bf16[288,1152]{1,0:T(8,128)(2,1)}, u32[]{:S(2)}, u32[]{:S(2)}) collective-permute-start(bf16[288,1152]{1,0:T(8,128)(2,1)} %get-tuple-element.206), channel_id=1, source_target_pairs={{0,4},{4,0},{1,5},{5,1},{2,6},{6,2},{3,7},{7,3},{8,12},{12,8},{9,1... | collective-permute-start | bytes 1990664 | tf_op jit(solution)/shard_map/ppermute | solution.py:21
  51.1 29.0 %collective-permute-start.10 = (bf16[512,2304]{1,0:T(8,128)(2,1)S(1)}, bf16[512,2304]{1,0:T(8,128)(2,1)}, u32[]{:S(2)}, u32[]{:S(2)}) collective-permute-start(bf16[512,2304]{1,0:T(8,128)(2,1)S(1)} %shard_map.356.refs_0_), channel_id=1, source_target_pairs={{0,1},{1,0},{2,3},{3,2},{4,5},{5,4},{6,7},{7,6},{8,9},{9,8},{10,11... | collective-permute-start | bytes 7077896 | tf_op jit(solution)/shard_map/ppermute | solution.py:21
  53.0 22.8 %collective-permute-start.11 = (bf16[288,1152]{1,0:T(8,128)(2,1)}, bf16[288,1152]{1,0:T(8,128)(2,1)}, u32[]{:S(2)}, u32[]{:S(2)}) collective-permute-start(bf16[288,1152]{1,0:T(8,128)(2,1)} %get-tuple-element.204), channel_id=1, source_target_pairs={{0,4},{4,0},{1,5},{5,1},{2,6},{6,2},{3,7},{7,3},{8,12},{12,8},{9,1... | collective-permute-start | bytes 1990664 | tf_op jit(solution)/shard_map/ppermute | solution.py:21
  54.6 18.0 %collective-permute-start = (s32[512]{0:T(512)S(1)}, s32[512]{0:T(512)S(1)}, u32[]{:S(2)}, u32[]{:S(2)}) collective-permute-start(s32[512]{0:T(512)S(1)} %copy-done.84), channel_id=1, source_target_pairs={{0,4},{4,0},{1,5},{5,1},{2,6},{6,2},{3,7},{7,3},{8,12},{12,8},{9,1... | collective-permute-start | bytes 6152 | tf_op jit(solution)/shard_map/ppermute | solution.py:21
  94.8 316.9 %all-gather.8.cloned.1.call-start = ((), (), s32[]{:S(2)}) async-start(), calls=%async_computation.5 | async-start | bytes 6635520 | tf_op jit(solution)/shard_map/all_gather | solution.py:366
  103.2 23.4 %collective-permute-start.13 = (bf16[1024,256]{1,0:T(8,128)(2,1)S(1)}, bf16[1024,256]{1,0:T(8,128)(2,1)S(1)}, u32[]{:S(2)}, u32[]{:S(2)}) collective-permute-start(bf16[1024,256]{1,0:T(8,128)(2,1)S(1)} %fusion.46), channel_id=1, source_target_pairs={{0,8},{8,16},{16,24},{1,9},{9,17},{17,25},{2,10},{10,18},{18,26},{... | collective-permute-start | bytes 1572872 | tf_op jit(solution)/shard_map/ppermute | solution.py:27
  104.5 22.0 %collective-permute-start.14 = (bf16[1024,256]{1,0:T(8,128)(2,1)S(1)}, bf16[1024,256]{1,0:T(8,128)(2,1)S(1)}, u32[]{:S(2)}, u32[]{:S(2)}) collective-permute-start(bf16[1024,256]{1,0:T(8,128)(2,1)S(1)} %fusion.46), channel_id=1, source_target_pairs={{0,4},{4,0},{1,5},{5,1},{2,6},{6,2},{3,7},{7,3},{8,12},{12,8},{9,1... | collective-permute-start | bytes 1572872 | tf_op jit(solution)/shard_map/ppermute | solution.py:21
  180.8 23.4 %collective-permute-start.21 = (bf16[2,128,1152]{2,1,0:T(8,128)(2,1)S(1)}, bf16[2,128,1152]{2,1,0:T(8,128)(2,1)S(1)}, u32[]{:S(2)}, u32[]{:S(2)}) collective-permute-start(bf16[2,128,1152]{2,1,0:T(8,128)(2,1)S(1)} %slice_bitcast_fusion.17), channel_id=1, source_target_pairs={{0,4},{4,0},{1,5},{5,1},{2,6},{6,2},{3,7},{7,3},{8,12},{12,8},{9,1... | collective-permute-start | bytes 1769480 | tf_op jit(solution)/shard_map/ppermute | solution.py:21
  182.2 22.0 %collective-permute-start.23 = (bf16[2,128,1152]{2,1,0:T(8,128)(2,1)S(1)}, bf16[2,128,1152]{2,1,0:T(8,128)(2,1)S(1)}, u32[]{:S(2)}, u32[]{:S(2)}) collective-permute-start(bf16[2,128,1152]{2,1,0:T(8,128)(2,1)S(1)} %slice_bitcast_fusion.15), channel_id=1, source_target_pairs={{0,2},{2,0},{1,3},{3,1},{4,6},{6,4},{5,7},{7,5},{8,10},{10,8},{9,1... | collective-permute-start | bytes 1769480 | tf_op jit(solution)/shard_map/ppermute | solution.py:21
  288.5 287.4 %reduce-scatter.4.cloned.1.call-start = ((), (), s32[]{:S(2)}) async-start(), calls=%async_computation.6 | async-start | bytes 6635520 | tf_op jit(solution)/shard_map/reduce_scatter | solution.py:449
  483.6 308.3 %reduce-scatter.6.cloned.1.call-start = ((), (), s32[]{:S(2)}) async-start(), calls=%async_computation.7 | async-start | bytes 13271040 | tf_op jit(solution)/shard_map/reduce_scatter | solution.py:449
  524.4 23.2 %collective-permute-start.45 = (bf16[512,2304]{1,0:T(8,128)(2,1)S(1)}, bf16[512,2304]{1,0:T(8,128)(2,1)}, u32[]{:S(2)}, u32[]{:S(2)}) collective-permute-start(bf16[512,2304]{1,0:T(8,128)(2,1)S(1)} %split.25), channel_id=1, source_target_pairs={{0,1},{1,0},{2,3},{3,2},{4,5},{5,4},{6,7},{7,6},{8,9},{9,8},{10,11... | collective-permute-start | bytes 7077896 | tf_op jit(solution)/shard_map/ppermute | solution.py:21
  577.3 288.8 %reduce-scatter.8.cloned.1.call-start = ((), (), s32[]{:S(2)}) async-start(), calls=%async_computation.8 | async-start | bytes 4423680 | tf_op jit(solution)/shard_map/reduce_scatter | solution.py:449
  609.2 25.6 %collective-permute-start.52 = (bf16[128,2304]{1,0:T(8,128)(2,1)S(1)}, bf16[128,2304]{1,0:T(8,128)(2,1)S(1)}, u32[]{:S(2)}, u32[]{:S(2)}) collective-permute-start(bf16[128,2304]{1,0:T(8,128)(2,1)S(1)} %get-tuple-element.188.refs_0_), channel_id=1, source_target_pairs={{0,6},{2,4},{4,2},{6,0},{1,7},{3,5},{5,3},{7,1},{8,14},{10,12},{12... | collective-permute-start | bytes 1769480 | tf_op jit(solution)/shard_map/ppermute | solution.py:136
  670.8 19.5 %collective-permute-start.56 = (bf16[1024,256]{1,0:T(8,128)(2,1)S(1)}, bf16[1024,256]{1,0:T(8,128)(2,1)S(1)}, u32[]{:S(2)}, u32[]{:S(2)}) collective-permute-start(bf16[1024,256]{1,0:T(8,128)(2,1)S(1)} %get-tuple-element.192), channel_id=1, source_target_pairs={{0,4},{4,0},{1,5},{5,1},{2,6},{6,2},{3,7},{7,3},{8,12},{12,8},{9,1... | collective-permute-start | bytes 1572872 | tf_op jit(solution)/shard_map/ppermute | solution.py:21
  679.8 21.6 %collective-permute-start.55 = (bf16[1024,256]{1,0:T(8,128)(2,1)}, bf16[1024,256]{1,0:T(8,128)(2,1)S(1)}, u32[]{:S(2)}, u32[]{:S(2)}) collective-permute-start(bf16[1024,256]{1,0:T(8,128)(2,1)} %get-tuple-element.193), channel_id=1, source_target_pairs={{0,4},{4,0},{1,5},{5,1},{2,6},{6,2},{3,7},{7,3},{8,12},{12,8},{9,1... | collective-permute-start | bytes 1572872 | tf_op jit(solution)/shard_map/ppermute | solution.py:21
  693.4 83.9 %collective-permute-start.61 = (bf16[288,1152]{1,0:T(8,128)(2,1)}, bf16[288,1152]{1,0:T(8,128)(2,1)}, u32[]{:S(2)}, u32[]{:S(2)}) collective-permute-start(bf16[288,1152]{1,0:T(8,128)(2,1)} %constant_dynamic-slice_fusion.2), channel_id=1, source_target_pairs={{0,4},{4,0},{1,5},{5,1},{2,6},{6,2},{3,7},{7,3},{8,12},{12,8},{9,1... | collective-permute-start | bytes 1990664 | tf_op jit(solution)/shard_map/ppermute | solution.py:21
  696.8 29.7 %collective-permute-start.54 = (bf16[1024,256]{1,0:T(8,128)(2,1)}, bf16[1024,256]{1,0:T(8,128)(2,1)S(1)}, u32[]{:S(2)}, u32[]{:S(2)}) collective-permute-start(bf16[1024,256]{1,0:T(8,128)(2,1)} %get-tuple-element.190), channel_id=1, source_target_pairs={{0,4},{4,0},{1,5},{5,1},{2,6},{6,2},{3,7},{7,3},{8,12},{12,8},{9,1... | collective-permute-start | bytes 1572872 | tf_op jit(solution)/shard_map/ppermute | solution.py:21
  703.0 63.5 %collective-permute-start.60 = (bf16[1024,256]{1,0:T(8,128)(2,1)S(1)}, bf16[1024,256]{1,0:T(8,128)(2,1)S(1)}, u32[]{:S(2)}, u32[]{:S(2)}) collective-permute-start(bf16[1024,256]{1,0:T(8,128)(2,1)S(1)} %fusion.44), channel_id=1, source_target_pairs={{8,0},{16,8},{24,16},{9,1},{17,9},{25,17},{10,2},{18,10},{26,18},{... | collective-permute-start | bytes 1572872 | tf_op jit(solution)/shard_map/ppermute | solution.py:27
  794.3 34.1 %collective-permute-start.62 = (bf16[288,2304]{1,0:T(8,128)(2,1)}, bf16[288,2304]{1,0:T(8,128)(2,1)S(1)}, u32[]{:S(2)}, u32[]{:S(2)}) collective-permute-start(bf16[288,2304]{1,0:T(8,128)(2,1)} %constant_dynamic-slice_fusion.1), channel_id=1, source_target_pairs={{0,4},{4,0},{1,5},{5,1},{2,6},{6,2},{3,7},{7,3},{8,12},{12,8},{9,1... | collective-permute-start | bytes 3981320 | tf_op jit(solution)/shard_map/ppermute | solution.py:21
  801.9 26.5 %collective-permute-start.63 = (f32[36352]{0:T(1024)S(1)}, f32[36352]{0:T(1024)S(1)}, u32[]{:S(2)}, u32[]{:S(2)}) collective-permute-start(f32[36352]{0:T(1024)S(1)} %divide_dynamic-update-slice_fusion), channel_id=1, source_target_pairs={{0,4},{4,0},{1,5},{5,1},{2,6},{6,2},{3,7},{7,3},{8,12},{12,8},{9,1... | collective-permute-start | bytes 436232 | tf_op jit(solution)/shard_map/ppermute | solution.py:21
  837.8 28.0 %collective-permute-start.65 = (bf16[2,128,2304]{2,1,0:T(8,128)(2,1)S(1)}, bf16[2,128,2304]{2,1,0:T(8,128)(2,1)S(1)}, u32[]{:S(2)}, u32[]{:S(2)}) collective-permute-start(bf16[2,128,2304]{2,1,0:T(8,128)(2,1)S(1)} %bitcast.150), channel_id=1, source_target_pairs={{0,4},{4,0},{1,5},{5,1},{2,6},{6,2},{3,7},{7,3},{8,12},{12,8},{9,1... | collective-permute-start | bytes 3538952 | tf_op jit(solution)/shard_map/ppermute | solution.py:21
  (156 other events, 2028.4 us)
Sparse Core Ops, SparseCore 0:
  23.2 71.4 all-gather.3
  96.9 190.1 all-gather.5
  288.7 122.8 all-gather.7
  483.7 92.1 reduce-scatter.3
  578.2 213.5 reduce-scatter.5
  795.9 70.0 reduce-scatter.7
